TPU v7x, 256 devices: a whole 4x4x8 slice. The times are simulated.
256 devices in a mesh: ctx: 64 (over x_hi, z, y), head: 4 (over x_lo, core).
Axes of the slice: x: 4 (x_hi: 2, x_lo: 2; x = x_hi * 2 + x_lo), y: 4, z: 8, core: 2. Of those that a mesh axis runs over, the one named last changes fastest.
Arguments:
- queries: bfloat16 [32768, 3072], P(('ctx', 'head')), may hold values from -6 to 6
- keys: bfloat16 [32768, 3072], P(('ctx', 'head')), may hold values from -6 to 6
- values: bfloat16 [32768, 3072], P(('ctx', 'head')), may hold values from -6 to 6
- outputs: bfloat16 [32768, 3072], P(('ctx', 'head')), may hold values from -4 to 4
- out_grads: bfloat16 [32768, 3072], P(('ctx', 'head')), may hold values from -6 to 6
- log_sums: float32 [32768, 24], P(('ctx', 'head')), may hold values from 2.5 to 4.5
- window_mask: int32 [128, 5], replicated, may hold values 0 or 1
- context_flag: int32 [128], replicated, may hold values 0 or 1
Outputs:
- query_grads: bfloat16 [32768, 3072], P(('ctx', 'head'))
- key_grads: bfloat16 [32768, 3072], P(('ctx', 'head'))
- value_grads: bfloat16 [32768, 3072], P(('ctx', 'head'))
All inputs are finite; a program needn't handle non-finite values.
Results may differ from a plain program's by a relative error of at most 0.0046.
The roundings to bfloat16 on the way count: a program that leaves them out, or rounds other values in their place, can miss the bound.
Values may be sent and summed in bfloat16 or wider, within the bound.
A program may use at most 128 MiB of HBM per device.

v0:
```python
import jax
import jax.numpy as jnp
from jax import lax
from jax.sharding import PartitionSpec as P

TILE_TOKENS = 256
WIN = 2


def with_halo(cells, sides, width):
    for axis, dim in sides:
        count = lax.axis_size(axis)
        head = lax.slice_in_dim(cells, 0, width, axis=dim)
        tail = lax.slice_in_dim(cells, cells.shape[dim] - width, cells.shape[dim], axis=dim)
        cells = jnp.concatenate(
            [
                lax.ppermute(tail, axis, [(i, (i + 1) % count) for i in range(count)]),
                cells,
                lax.ppermute(head, axis, [((i + 1) % count, i) for i in range(count)]),
            ],
            axis=dim,
        )
    return cells


def shifted(value, axis, steps):
    count = lax.axis_size(axis)
    pairs = [(source, (source + steps) % count) for source in range(count)]
    return lax.ppermute(value, axis, pairs)


def tile_allowed(query_tiles, key_tiles, window_mask, context_flag, total_tiles, reach):
    offset = (key_tiles[None, :] - query_tiles[:, None] + reach) % total_tiles
    inside = offset <= 2 * reach
    column = jnp.minimum(offset, 2 * reach)
    table = window_mask[query_tiles]
    picked = jnp.take_along_axis(table, column, axis=1)
    window_ok = (picked == 1) | (offset == reach)
    ctx_query = context_flag[query_tiles][:, None]
    ctx_key = context_flag[key_tiles][None, :]
    return inside & window_ok & ((ctx_query == 0) | (ctx_key == 1))


def expand_mask(allowed, tile):
    count_q, count_k = allowed.shape
    full = jnp.broadcast_to(allowed[:, None, :, None], (count_q, tile, count_k, tile))
    return full.reshape(count_q * tile, count_k * tile)


def block_grads(q_blk, do_blk, lse_blk, delta_blk, k_blk, v_blk, mask, scale):
    scores = jnp.einsum("qhd,khd->hqk", q_blk, k_blk, preferred_element_type=jnp.float32) * scale
    probs = jnp.where(mask[None], jnp.exp(scores - lse_blk.T[:, :, None]), jnp.float32(0.0))
    dprobs = jnp.einsum("qhd,khd->hqk", do_blk, v_blk, preferred_element_type=jnp.float32)
    dscores = probs * (dprobs - delta_blk.T[:, :, None])
    probs_b = probs.astype(jnp.bfloat16)
    dscores_b = dscores.astype(jnp.bfloat16)
    value_gradient = jnp.einsum("hqk,qhd->khd", probs_b, do_blk, preferred_element_type=jnp.float32)
    grad_k = (
        jnp.einsum("hqk,qhd->khd", dscores_b, q_blk, preferred_element_type=jnp.float32) * scale
    )
    query_gradient = (
        jnp.einsum("hqk,khd->qhd", dscores_b, k_blk, preferred_element_type=jnp.float32) * scale
    )
    return (query_gradient, grad_k, value_gradient)


def per_device(queries, keys, values, outputs, out_grads, log_sums, window_mask, context_flag):
    heads_all = log_sums.shape[1]
    head_size = queries.shape[1] // heads_all
    groups = lax.axis_size("head")
    heads_here = heads_all // groups
    scale = head_size ** (-0.5)
    tile_span = 2 * WIN + 1
    border_tiles = WIN * TILE_TOKENS
    q_in, k_in, v_in, o_in, do_in = (
        lax.all_to_all(queries, "head", split_axis=1, concat_axis=0, tiled=True),
        lax.all_to_all(keys, "head", split_axis=1, concat_axis=0, tiled=True),
        lax.all_to_all(values, "head", split_axis=1, concat_axis=0, tiled=True),
        lax.all_to_all(outputs, "head", split_axis=1, concat_axis=0, tiled=True),
        lax.all_to_all(out_grads, "head", split_axis=1, concat_axis=0, tiled=True),
    )
    lse_h = lax.all_to_all(log_sums, "head", split_axis=1, concat_axis=0, tiled=True)
    rows_now = q_in.shape[0]
    delta_h = jnp.einsum(
        "qhd,qhd->qh",
        do_in.reshape(rows_now, heads_here, head_size),
        o_in.reshape(rows_now, heads_here, head_size),
        preferred_element_type=jnp.float32,
    )
    row_range = q_in.shape[0]
    local_width = heads_here * head_size
    local_tiles = row_range // TILE_TOKENS
    total_tiles = local_tiles * lax.axis_size("ctx")
    first_tile = lax.axis_index("ctx") * local_tiles
    offsets = jnp.arange(tile_span, dtype=jnp.int32)
    q3 = q_in.reshape(row_range, heads_here, head_size)
    do3 = do_in.reshape(row_range, heads_here, head_size)
    wide = with_halo(jnp.stack([k_in, v_in]), (("ctx", 1),), border_tiles)
    key_ext = wide[0].reshape(row_range + 2 * border_tiles, heads_here, head_size)
    val_ext = wide[1].reshape(row_range + 2 * border_tiles, heads_here, head_size)

    def query_block(index):
        start_index = index * TILE_TOKENS
        q_blk = lax.dynamic_slice_in_dim(q3, start_index, TILE_TOKENS, 0)
        do_blk = lax.dynamic_slice_in_dim(do3, start_index, TILE_TOKENS, 0)
        lse_blk = lax.dynamic_slice_in_dim(lse_h, start_index, TILE_TOKENS, 0)
        delta_blk = lax.dynamic_slice_in_dim(delta_h, start_index, TILE_TOKENS, 0)
        k_blk = lax.dynamic_slice_in_dim(key_ext, start_index, tile_span * TILE_TOKENS, 0)
        v_blk = lax.dynamic_slice_in_dim(val_ext, start_index, tile_span * TILE_TOKENS, 0)
        query_tiles = jnp.reshape(first_tile + index, (1,))
        key_tiles = (first_tile + index - WIN + offsets) % total_tiles
        mask = expand_mask(
            tile_allowed(query_tiles, key_tiles, window_mask, context_flag, total_tiles, WIN),
            TILE_TOKENS,
        )
        return block_grads(q_blk, do_blk, lse_blk, delta_blk, k_blk, v_blk, mask, scale)

    query_zeros = jnp.zeros((row_range, heads_here, head_size), jnp.float32)
    extended_zeros = jnp.zeros((row_range + 2 * border_tiles, heads_here, head_size), jnp.float32)

    def complete_step(index, loop_carry):
        query_gradient, key_extended, value_extended = loop_carry
        start_index = index * TILE_TOKENS
        gq, gk, value_grad_block = query_block(index)
        query_gradient = lax.dynamic_update_slice_in_dim(query_gradient, gq, start_index, 0)
        old_k = lax.dynamic_slice_in_dim(key_extended, start_index, tile_span * TILE_TOKENS, 0)
        previous_value = lax.dynamic_slice_in_dim(
            value_extended, start_index, tile_span * TILE_TOKENS, 0
        )
        key_extended = lax.dynamic_update_slice_in_dim(key_extended, old_k + gk, start_index, 0)
        value_extended = lax.dynamic_update_slice_in_dim(
            value_extended, previous_value + value_grad_block, start_index, 0
        )
        return (query_gradient, key_extended, value_extended)

    query_gradient, key_extended, value_extended = lax.fori_loop(
        0, local_tiles, complete_step, (query_zeros, extended_zeros, extended_zeros)
    )
    key_extended = key_extended.reshape(row_range + 2 * border_tiles, local_width)
    value_extended = value_extended.reshape(row_range + 2 * border_tiles, local_width)
    left_portion = jnp.stack([key_extended[:border_tiles], value_extended[:border_tiles]])
    right_portion = jnp.stack(
        [key_extended[border_tiles + row_range :], value_extended[border_tiles + row_range :]]
    )
    from_right = shifted(left_portion, "ctx", -1)
    from_left = shifted(right_portion, "ctx", 1)
    grad_k = key_extended[border_tiles : border_tiles + row_range]
    value_gradient = value_extended[border_tiles : border_tiles + row_range]
    grad_k = (
        grad_k.at[:border_tiles].add(from_left[0]).at[row_range - border_tiles :].add(from_right[0])
    )
    value_gradient = (
        value_gradient.at[:border_tiles]
        .add(from_left[1])
        .at[row_range - border_tiles :]
        .add(from_right[1])
    )
    query_gradient = query_gradient.reshape(row_range, local_width).astype(jnp.bfloat16)
    grad_k = grad_k.astype(jnp.bfloat16)
    value_gradient = value_gradient.astype(jnp.bfloat16)
    query_grads, key_grads, value_grads = (
        lax.all_to_all(query_gradient, "head", split_axis=0, concat_axis=1, tiled=True),
        lax.all_to_all(grad_k, "head", split_axis=0, concat_axis=1, tiled=True),
        lax.all_to_all(value_gradient, "head", split_axis=0, concat_axis=1, tiled=True),
    )
    return (query_grads, key_grads, value_grads)


def solution(mesh):
    placed = (
        P(("ctx", "head"), None),
        P(("ctx", "head"), None),
        P(("ctx", "head"), None),
        P(("ctx", "head"), None),
        P(("ctx", "head"), None),
        P(("ctx", "head"), None),
        P(),
        P(),
    )
    return jax.shard_map(
        per_device,
        mesh=mesh,
        in_specs=placed,
        out_specs=(P(("ctx", "head"), None), P(("ctx", "head"), None), P(("ctx", "head"), None)),
        check_vma=False,
    )
```

profile of v0, /device:TPU:36, one launch (start us, length us, event | category | flops | bytes accessed | tf_op | source)
XLA Modules:
  0.0 300.3 jit_solution(15679963272215466955)
XLA Ops:
  0.7 2.4 copy.140
  3.1 3.5 %all-to-all-start = ((bf16[128,4,768]{0,2,1:T(8,128)(2,1)}), bf16[128,4,768]{0,2,1:T(8,128)(2,1)S(1)}, u32[]{:S(2)}, u32[]{:S(2)}) async-start(bf16[128,4,768]{0,2,1:T(8,128)(2,1)} %bitcast), calls=%async_computation | async-start | bytes 1572864 | tf_op jit(solution)/shard_map/all_to_all | solution.py:77
  7.7 10.5 %all-to-all-done = bf16[128,4,768]{0,2,1:T(8,128)(2,1)S(1)} async-done(((bf16[128,4,768]{0,2,1:T(8,128)(2,1)}), bf16[128,4,768]{0,2,1:T(8,128)(2,1)S(1)}, u32[]{:S(2)}, u32[]{:S(2)}) %all-to-all-start) | async-done | bytes 786464 | tf_op jit(solution)/shard_map/all_to_all | solution.py:77
  18.2 3.5 %all-to-all-start.1 = ((bf16[128,4,768]{0,2,1:T(8,128)(2,1)}), bf16[128,4,768]{0,2,1:T(8,128)(2,1)S(1)}, u32[]{:S(2)}, u32[]{:S(2)}) async-start(bf16[128,4,768]{0,2,1:T(8,128)(2,1)} %bitcast.3), calls=%async_computation.1 | async-start | bytes 1572864 | tf_op jit(solution)/shard_map/all_to_all | solution.py:78
  22.8 10.5 %all-to-all-done.1 = bf16[128,4,768]{0,2,1:T(8,128)(2,1)S(1)} async-done(((bf16[128,4,768]{0,2,1:T(8,128)(2,1)}), bf16[128,4,768]{0,2,1:T(8,128)(2,1)S(1)}, u32[]{:S(2)}, u32[]{:S(2)}) %all-to-all-start.1) | async-done | bytes 786464 | tf_op jit(solution)/shard_map/all_to_all | solution.py:78
  33.3 3.5 %all-to-all-start.2 = ((bf16[128,4,768]{0,2,1:T(8,128)(2,1)}), bf16[128,4,768]{0,2,1:T(8,128)(2,1)S(1)}, u32[]{:S(2)}, u32[]{:S(2)}) async-start(bf16[128,4,768]{0,2,1:T(8,128)(2,1)} %bitcast.7), calls=%async_computation.2 | async-start | bytes 1572864 | tf_op jit(solution)/shard_map/all_to_all | solution.py:76
  39.9 2.6 collective-permute-start.1
  43.6 4.8 %all-to-all-done.2 = bf16[128,4,768]{0,2,1:T(8,128)(2,1)S(1)} async-done(((bf16[128,4,768]{0,2,1:T(8,128)(2,1)}), bf16[128,4,768]{0,2,1:T(8,128)(2,1)S(1)}, u32[]{:S(2)}, u32[]{:S(2)}) %all-to-all-start.2) | async-done | bytes 786464 | tf_op jit(solution)/shard_map/all_to_all | solution.py:76
  48.4 3.5 %all-to-all-start.5 = ((bf16[128,4,768]{0,2,1:T(8,128)(2,1)}), bf16[128,4,768]{0,2,1:T(8,128)(2,1)S(1)}, u32[]{:S(2)}, u32[]{:S(2)}) async-start(bf16[128,4,768]{0,2,1:T(8,128)(2,1)} %bitcast.129), calls=%async_computation.5 | async-start | bytes 1572864 | tf_op jit(solution)/shard_map/all_to_all | solution.py:79
  51.9 2.3 copy.147
  54.2 9.3 %all-to-all-done.5 = bf16[128,4,768]{0,2,1:T(8,128)(2,1)S(1)} async-done(((bf16[128,4,768]{0,2,1:T(8,128)(2,1)}), bf16[128,4,768]{0,2,1:T(8,128)(2,1)S(1)}, u32[]{:S(2)}, u32[]{:S(2)}) %all-to-all-start.5) | async-done | bytes 786464 | tf_op jit(solution)/shard_map/all_to_all | solution.py:79
  64.4 3.5 %all-to-all-start.4 = ((bf16[128,4,768]{0,2,1:T(8,128)(2,1)}), bf16[128,4,768]{0,2,1:T(8,128)(2,1)S(1)}, u32[]{:S(2)}, u32[]{:S(2)}) async-start(bf16[128,4,768]{0,2,1:T(8,128)(2,1)} %bitcast.125), calls=%async_computation.4 | async-start | bytes 1572864 | tf_op jit(solution)/shard_map/all_to_all | solution.py:80
  71.8 2.6 copy.151
  74.4 2.3 reshape.415
  76.8 2.8 all-to-all-done.4
  79.5 3.4 %all-to-all-start.3 = ((f32[128,4,6]{0,2,1:T(8,128)}), f32[128,4,6]{0,2,1:T(8,128)S(1)}, u32[]{:S(2)}, u32[]{:S(2)}) async-start(f32[128,4,6]{0,2,1:T(8,128)} %all_to_all.119), calls=%async_computation.3 | async-start | bytes 32768 | tf_op jit(solution)/shard_map/all_to_all | solution.py:82
  87.8 2.2 pad_maximum_fusion
  90.0 2.5 fusion.51
  92.5 4.3 %copy.149 = bf16[1,1536,768]{1,2,0:T(8,128)(2,1)} copy(bf16[1,1536,768]{2,1,0:T(8,128)(2,1)} %get-tuple-element.596) | data formatting | bytes 4718592 | tf_op jit(solution)/shard_map/slice | solution.py:100
  96.7 2.8 copy.144
  100.5 2.8 broadcast_in_dim.91.clone
  103.3 2.8 broadcast_in_dim.91
  106.1 30.6 %while.30 = (s32[]{:T(128)}, bf16[512,6,128]{0,2,1:T(8,128)(2,1)}, f32[1536,6,128]{0,2,1:T(8,128)}, f32[1536,6,128]{0,2,1:T(8,128)}, bf16[1536,6,128]{0,2,1:T(8,...) while((s32[]{:T(128)}, bf16[512,6,128]{0,2,1:T(8,128)(2,1)}, ...), condition=%wide.region_1.2_spmd.clone, body=%wide.region_0.1_spmd.clone.sunk | while | flops 2539391488 | bytes 144376496 | solution.py:136
  110.6 2.7 multiply_convert_fusion.2
  113.3 2.2 fusion.87
  119.2 2.2 copy-done.1
  125.9 2.7 multiply_convert_fusion.2
  128.6 2.2 fusion.87
  134.6 2.2 copy-done.1
  136.7 5.0 %fusion.49 = (f32[512,6,128]{0,2,1:T(8,128)S(1)}, f32[512,6,128]{0,2,1:T(8,128)S(1)}, f32[512,6,128]{0,2,1:T(8,128)S(1)}, f32[512,6,128]{0,2,1:T(8,128)S(1)}, f3...) fusion(f32[1536,6,128]{0,2,1:T(8,128)} %get-tuple-element.419, f32[1536,6,128]{0,2,1:T(8,128)} %get-tuple-element.418), kind=kLoop, calls=%fused_computation.76 | loop fusion | bytes 18874368 | tf_op jit(solution)/shard_map/slice | solution.py:148
  141.7 2.0 pad_maximum_fusion.1
  147.3 34.7 %collective-permute-start.3 = (f32[2,512,768]{1,2,0:T(8,128)}, f32[2,512,768]{1,2,0:T(8,128)}, u32[]{:S(2)}, u32[]{:S(2)}) collective-permute-start(f32[2,512,768]{1,2,0:T(8,128)} %pad_maximum_fusion.2), channel_id=1, source_target_pairs={{0,252},{4,0},{8,4},{12,8},{16,12},{20,16},{24,20},{28,24},{32,28}... | collective-permute-start | bytes 9437192 | tf_op jit(solution)/shard_map/ppermute | solution.py:29
  185.3 2.4 convert_element_type.36
  187.8 2.2 copy.157
  190.0 4.2 %all-to-all-start.6 = ((bf16[4,128,768]{2,1,0:T(8,128)(2,1)}), bf16[4,128,768]{2,1,0:T(8,128)(2,1)}, u32[]{:S(2)}, u32[]{:S(2)}) async-start(bf16[4,128,768]{2,1,0:T(8,128)(2,1)} %copy.157), calls=%async_computation.6 | async-start | bytes 1572864 | tf_op jit(solution)/shard_map/all_to_all | solution.py:162
  194.2 54.7 %collective-permute-done.2 = f32[2,512,768]{1,2,0:T(8,128)} collective-permute-done((f32[2,512,768]{1,2,0:T(8,128)}, f32[2,512,768]{1,2,0:T(8,128)}, u32[]{:S(2)}, u32[]{:S(2)}) %collective-permute-start.2) | collective-permute-done | bytes 3145760 | tf_op jit(solution)/shard_map/ppermute | solution.py:29
  248.9 3.9 %fusion.52 = (f32[1,512,768]{1,2,0:T(8,128)}, f32[1,512,768]{1,2,0:T(8,128)}) fusion(f32[2,512,768]{1,2,0:T(8,128)} %collective-permute-done.2), kind=kLoop, calls=%fused_computation.79 | loop fusion | bytes 6291456 | tf_op jit(solution)/shard_map/slice | solution.py:154
  252.7 3.1 %copy.163 = f32[1,512,768]{2,1,0:T(8,128)} copy(f32[1,512,768]{1,2,0:T(8,128)} %get-tuple-element.598) | data formatting | bytes 3145728 | tf_op jit(solution)/shard_map/slice | solution.py:154
  255.8 3.9 %fusion.53 = (f32[1,512,768]{1,2,0:T(8,128)}, f32[1,512,768]{1,2,0:T(8,128)}) fusion(f32[2,512,768]{1,2,0:T(8,128)} %collective-permute-done.3), kind=kLoop, calls=%fused_computation.80 | loop fusion | bytes 6291456 | tf_op jit(solution)/shard_map/slice | solution.py:156
  259.7 3.1 %copy.165 = f32[1,512,768]{2,1,0:T(8,128)} copy(f32[1,512,768]{1,2,0:T(8,128)} %get-tuple-element.600) | data formatting | bytes 3145728 | tf_op jit(solution)/shard_map/slice | solution.py:156
  262.8 3.0 add_convert_fusion
  265.8 2.3 copy.166
  268.1 4.2 %all-to-all-start.8 = ((bf16[4,128,768]{1,2,0:T(8,128)(2,1)}), bf16[4,128,768]{1,2,0:T(8,128)(2,1)}, u32[]{:S(2)}, u32[]{:S(2)}) async-start(bf16[4,128,768]{1,2,0:T(8,128)(2,1)} %copy.166), calls=%async_computation.8 | async-start | bytes 1572864 | tf_op jit(solution)/shard_map/all_to_all | solution.py:164
  277.7 2.1 add_convert_fusion.1
  281.0 3.0 %all-to-all-done.8 = bf16[4,128,768]{1,2,0:T(8,128)(2,1)} async-done(((bf16[4,128,768]{1,2,0:T(8,128)(2,1)}), bf16[4,128,768]{1,2,0:T(8,128)(2,1)}, u32[]{:S(2)}, u32[]{:S(2)}) %all-to-all-start.8) | async-done | bytes 786464 | tf_op jit(solution)/shard_map/all_to_all | solution.py:164
  284.0 3.5 %all-to-all-start.7 = ((bf16[4,128,768]{1,2,0:T(8,128)(2,1)}), bf16[4,128,768]{1,2,0:T(8,128)(2,1)S(1)}, u32[]{:S(2)}, u32[]{:S(2)}) async-start(bf16[4,128,768]{1,2,0:T(8,128)(2,1)} %copy.162), calls=%async_computation.7 | async-start | bytes 1572864 | tf_op jit(solution)/shard_map/all_to_all | solution.py:163
  290.2 2.3 copy.169
  292.4 6.7 %all-to-all-done.7 = bf16[4,128,768]{1,2,0:T(8,128)(2,1)S(1)} async-done(((bf16[4,128,768]{1,2,0:T(8,128)(2,1)}), bf16[4,128,768]{1,2,0:T(8,128)(2,1)S(1)}, u32[]{:S(2)}, u32[]{:S(2)}) %all-to-all-start.7) | async-done | bytes 786464 | tf_op jit(solution)/shard_map/all_to_all | solution.py:163
  (126 shorter events, 49.5 us)
Async XLA Ops:
  0.6 5.9 %copy-start.13 = (bf16[128,3072]{1,0:T(8,128)(2,1)S(1)}, bf16[128,3072]{1,0:T(8,128)(2,1)}, u32[]{:S(2)}) copy-start(bf16[128,3072]{1,0:T(8,128)(2,1)} %param.28) | copy-start | bytes 2359300
  0.6 21.0 %copy-start.14 = (bf16[128,3072]{1,0:T(8,128)(2,1)S(1)}, bf16[128,3072]{1,0:T(8,128)(2,1)}, u32[]{:S(2)}) copy-start(bf16[128,3072]{1,0:T(8,128)(2,1)} %param.26) | copy-start | bytes 2359300
  3.1 15.1 %all-to-all-start = ((bf16[128,4,768]{0,2,1:T(8,128)(2,1)}), bf16[128,4,768]{0,2,1:T(8,128)(2,1)S(1)}, u32[]{:S(2)}, u32[]{:S(2)}) async-start(bf16[128,4,768]{0,2,1:T(8,128)(2,1)} %bitcast), calls=%async_computation | async-start | bytes 1572864 | tf_op jit(solution)/shard_map/all_to_all | solution.py:77
  18.2 15.1 %all-to-all-start.1 = ((bf16[128,4,768]{0,2,1:T(8,128)(2,1)}), bf16[128,4,768]{0,2,1:T(8,128)(2,1)S(1)}, u32[]{:S(2)}, u32[]{:S(2)}) async-start(bf16[128,4,768]{0,2,1:T(8,128)(2,1)} %bitcast.3), calls=%async_computation.1 | async-start | bytes 1572864 | tf_op jit(solution)/shard_map/all_to_all | solution.py:78
  33.3 3.8 %copy-start.9 = (bf16[128,4,768]{0,2,1:T(8,128)(2,1)}, bf16[128,4,768]{0,2,1:T(8,128)(2,1)S(1)}, u32[]{:S(2)}) copy-start(bf16[128,4,768]{0,2,1:T(8,128)(2,1)S(1)} %all-to-all-done.1) | copy-start | bytes 2359300
  33.3 15.1 %all-to-all-start.2 = ((bf16[128,4,768]{0,2,1:T(8,128)(2,1)}), bf16[128,4,768]{0,2,1:T(8,128)(2,1)S(1)}, u32[]{:S(2)}, u32[]{:S(2)}) async-start(bf16[128,4,768]{0,2,1:T(8,128)(2,1)} %bitcast.7), calls=%async_computation.2 | async-start | bytes 1572864 | tf_op jit(solution)/shard_map/all_to_all | solution.py:76
  37.1 5.4 %copy-start.15 = (bf16[128,3072]{1,0:T(8,128)(2,1)S(1)}, bf16[128,3072]{1,0:T(8,128)(2,1)}, u32[]{:S(2)}) copy-start(bf16[128,3072]{1,0:T(8,128)(2,1)} %param.29) | copy-start | bytes 2359300
  39.9 28.0 %copy-start.16 = (f32[128,24]{0,1:T(8,128)S(1)}, f32[128,24]{0,1:T(8,128)}, u32[]{:S(2)}) copy-start(f32[128,24]{0,1:T(8,128)} %param.31) | copy-start | bytes 36868
  39.9 28.6 %copy-start.17 = (s32[128,5]{0,1:T(8,128)S(1)}, s32[128,5]{0,1:T(8,128)}, u32[]{:S(2)}) copy-start(s32[128,5]{0,1:T(8,128)} %param.32) | copy-start | bytes 7684
  39.9 47.9 %collective-permute-start.1 = (bf16[2,512,768]{2,1,0:T(8,128)(2,1)}, bf16[2,512,768]{2,1,0:T(8,128)(2,1)}, u32[]{:S(2)}, u32[]{:S(2)}) collective-permute-start(bf16[2,512,768]{2,1,0:T(8,128)(2,1)} %pad_maximum_fusion.3), channel_id=1, source_target_pairs={{4,0},{8,4},{12,8},{16,12},{20,16},{24,20},{28,24},{32,28},{36,32}... | collective-permute-start | bytes 4718600 | tf_op jit(solution)/shard_map/ppermute | solution.py:19
  42.5 45.3 %collective-permute-start = (bf16[2,512,768]{2,1,0:T(8,128)(2,1)}, bf16[2,512,768]{2,1,0:T(8,128)(2,1)}, u32[]{:S(2)}, u32[]{:S(2)}) collective-permute-start(bf16[2,512,768]{2,1,0:T(8,128)(2,1)} %pad_maximum_fusion.3), channel_id=1, source_target_pairs={{0,4},{4,8},{8,12},{12,16},{16,20},{20,24},{24,28},{28,32},{32,36}... | collective-permute-start | bytes 4718600 | tf_op jit(solution)/shard_map/ppermute | solution.py:17
  48.4 15.1 %all-to-all-start.5 = ((bf16[128,4,768]{0,2,1:T(8,128)(2,1)}), bf16[128,4,768]{0,2,1:T(8,128)(2,1)S(1)}, u32[]{:S(2)}, u32[]{:S(2)}) async-start(bf16[128,4,768]{0,2,1:T(8,128)(2,1)} %bitcast.129), calls=%async_computation.5 | async-start | bytes 1572864 | tf_op jit(solution)/shard_map/all_to_all | solution.py:79
  63.5 0.9 copy-start.8
  64.4 15.1 %all-to-all-start.4 = ((bf16[128,4,768]{0,2,1:T(8,128)(2,1)}), bf16[128,4,768]{0,2,1:T(8,128)(2,1)S(1)}, u32[]{:S(2)}, u32[]{:S(2)}) async-start(bf16[128,4,768]{0,2,1:T(8,128)(2,1)} %bitcast.125), calls=%async_computation.4 | async-start | bytes 1572864 | tf_op jit(solution)/shard_map/all_to_all | solution.py:80
  79.5 20.0 %all-to-all-start.3 = ((f32[128,4,6]{0,2,1:T(8,128)}), f32[128,4,6]{0,2,1:T(8,128)S(1)}, u32[]{:S(2)}, u32[]{:S(2)}) async-start(f32[128,4,6]{0,2,1:T(8,128)} %all_to_all.119), calls=%async_computation.3 | async-start | bytes 32768 | tf_op jit(solution)/shard_map/all_to_all | solution.py:82
  86.1 3.9 %copy-start.3 = (bf16[512,6,128]{0,2,1:T(8,128)(2,1)}, bf16[512,6,128]{0,2,1:T(8,128)(2,1)S(1)}, u32[]{:S(2)}) copy-start(bf16[512,6,128]{0,2,1:T(8,128)(2,1)S(1)} %reshape.414) | copy-start | bytes 2359300
  103.3 2.8 copy-start
  108.7 1.3 copy-start.4
  108.7 1.9 copy-start.12
  108.7 4.6 %slice-start.2 = ((s8[4718592]{0:T(1024)(128)(4,1)}), s8[4194304]{0:T(1024)(128)(4,1)S(1)}, s32[]{:S(2)}) async-start(s8[4718592]{0:T(1024)(128)(4,1)} %bitcast.108), calls=%async_computation.11 | async-start | bytes 8388608 | tf_op jit(solution)/shard_map/while
  110.6 2.7 slice-start.3
  110.6 7.1 %slice-start = ((s8[4718592]{0:T(1024)(128)(4,1)}), s8[4194304]{0:T(1024)(128)(4,1)S(1)}, s32[]{:S(2)}) async-start(s8[4718592]{0:T(1024)(128)(4,1)} %bitcast.106), calls=%async_computation.9 | async-start | bytes 8388608 | tf_op jit(solution)/shard_map/while
  113.3 2.2 copy-start.10
  113.3 4.4 %slice-start.1 = ((s8[4718592]{0:T(1024)(128)(4,1)}), s8[524288]{0:T(1024)(128)(4,1)S(1)}, s32[]{:S(2)}) async-start(s8[4718592]{0:T(1024)(128)(4,1)} %bitcast.106), calls=%async_computation.10 | async-start | bytes 1048576 | tf_op jit(solution)/shard_map/while
  115.5 2.2 copy-start.2
  117.7 1.5 copy-start.11
  119.2 2.2 copy-start.1
  124.0 1.3 copy-start.4
  124.0 1.9 copy-start.12
  124.0 4.6 %slice-start.2 = ((s8[4718592]{0:T(1024)(128)(4,1)}), s8[4194304]{0:T(1024)(128)(4,1)S(1)}, s32[]{:S(2)}) async-start(s8[4718592]{0:T(1024)(128)(4,1)} %bitcast.108), calls=%async_computation.11 | async-start | bytes 8388608 | tf_op jit(solution)/shard_map/while
  125.9 2.7 slice-start.3
  125.9 7.2 %slice-start = ((s8[4718592]{0:T(1024)(128)(4,1)}), s8[4194304]{0:T(1024)(128)(4,1)S(1)}, s32[]{:S(2)}) async-start(s8[4718592]{0:T(1024)(128)(4,1)} %bitcast.106), calls=%async_computation.9 | async-start | bytes 8388608 | tf_op jit(solution)/shard_map/while
  128.6 2.3 copy-start.10
  128.6 4.4 %slice-start.1 = ((s8[4718592]{0:T(1024)(128)(4,1)}), s8[524288]{0:T(1024)(128)(4,1)S(1)}, s32[]{:S(2)}) async-start(s8[4718592]{0:T(1024)(128)(4,1)} %bitcast.106), calls=%async_computation.10 | async-start | bytes 1048576 | tf_op jit(solution)/shard_map/while
  130.8 2.2 copy-start.2
  133.0 1.5 copy-start.11
  134.5 2.2 copy-start.1
  143.7 105.1 %collective-permute-start.2 = (f32[2,512,768]{1,2,0:T(8,128)}, f32[2,512,768]{1,2,0:T(8,128)}, u32[]{:S(2)}, u32[]{:S(2)}) collective-permute-start(f32[2,512,768]{1,2,0:T(8,128)} %pad_maximum_fusion.1), channel_id=1, source_target_pairs={{0,4},{4,8},{8,12},{12,16},{16,20},{20,24},{24,28},{28,32},{32,36}... | collective-permute-start | bytes 9437192 | tf_op jit(solution)/shard_map/ppermute | solution.py:29
  147.3 108.5 %collective-permute-start.3 = (f32[2,512,768]{1,2,0:T(8,128)}, f32[2,512,768]{1,2,0:T(8,128)}, u32[]{:S(2)}, u32[]{:S(2)}) collective-permute-start(f32[2,512,768]{1,2,0:T(8,128)} %pad_maximum_fusion.2), channel_id=1, source_target_pairs={{0,252},{4,0},{8,4},{12,8},{16,12},{20,16},{24,20},{28,24},{32,28}... | collective-permute-start | bytes 9437192 | tf_op jit(solution)/shard_map/ppermute | solution.py:29
  190.0 78.1 %all-to-all-start.6 = ((bf16[4,128,768]{2,1,0:T(8,128)(2,1)}), bf16[4,128,768]{2,1,0:T(8,128)(2,1)}, u32[]{:S(2)}, u32[]{:S(2)}) async-start(bf16[4,128,768]{2,1,0:T(8,128)(2,1)} %copy.157), calls=%async_computation.6 | async-start | bytes 1572864 | tf_op jit(solution)/shard_map/all_to_all | solution.py:162
  268.1 15.9 %all-to-all-start.8 = ((bf16[4,128,768]{1,2,0:T(8,128)(2,1)}), bf16[4,128,768]{1,2,0:T(8,128)(2,1)}, u32[]{:S(2)}, u32[]{:S(2)}) async-start(bf16[4,128,768]{1,2,0:T(8,128)(2,1)} %copy.166), calls=%async_computation.8 | async-start | bytes 1572864 | tf_op jit(solution)/shard_map/all_to_all | solution.py:164
  272.8 1.6 copy-start.5
  274.4 1.6 copy-start.6
  276.1 1.6 copy-start.7
  284.0 15.1 %all-to-all-start.7 = ((bf16[4,128,768]{1,2,0:T(8,128)(2,1)}), bf16[4,128,768]{1,2,0:T(8,128)(2,1)S(1)}, u32[]{:S(2)}, u32[]{:S(2)}) async-start(bf16[4,128,768]{1,2,0:T(8,128)(2,1)} %copy.162), calls=%async_computation.7 | async-start | bytes 1572864 | tf_op jit(solution)/shard_map/all_to_all | solution.py:163
where the time goes:
time: 302 us; the launch traced here: 300 us
  waiting for transfers between devices  102 us (34%)
  local copies, waits for them, and re-layouts  91.8 us (30%)
  starting transfers between devices  71.6 us (24%)
  matrix products  17.9 us (6%)
  other arithmetic  14.4 us (5%)
    ppermute x2, waiting for transfers between devices, shifted(): return lax.ppermute(value, axis, pairs)  54.7 us
    ppermute x2, starting transfers between devices, shifted(): return lax.ppermute(value, axis, pairs)  36.3 us
    unnamed x33, local copies, waits for them, and re-layouts  13.8 us
    all_to_all x1, waiting for transfers between devices, per_device(): lax.all_to_all(keys, 'head', split_axis=1, concat_axis=0, tiled=True)  10.5 us
    all_to_all x1, waiting for transfers between devices, per_device(): lax.all_to_all(values, 'head', split_axis=1, concat_axis=0, tiled=True)  10.5 us
    all_to_all x1, waiting for transfers between devices, per_device(): lax.all_to_all(outputs, 'head', split_axis=1, concat_axis=0, tiled=True)  9.33 us
    slice x3, local copies, waits for them, and re-layouts, per_device(): value_gradient = value_extended[border_tiles:border_tiles + row_range]  8.31 us
    while x40, local copies, waits for them, and re-layouts  7.22 us
  transfers between devices with their start and end apart: 13, of which 8 were waited for; matrix products, arithmetic and copies ran while one was open for 25% of the time, Pallas kernels for 0%

commit v1 on v0

v1 whole, which is shorter than its diff:
```python
import functools

import jax
import jax.numpy as jnp
from jax import lax
from jax.experimental import pallas as pl
from jax.experimental.pallas import tpu as pltpu
from jax.sharding import PartitionSpec as P

TILE = 256
HD = 128
WIN = 2
AHEAD = 2
LOG2E = 1.4426950408889634
OFF = 1e30
MESH = pl.DeviceIdType.MESH
NT = (((1,), (1,)), ((), ()))


def matmul(a, b):
    return jnp.dot(a, b, preferred_element_type=jnp.float32)


def kernel(
    ctx_count,
    heads,
    q_ref, k_ref, v_ref, o_ref, do_ref, lse_ref, wm_ref, cf_ref,
    dq_ref, dk_ref, dv_ref,
    own, halo, stat_send, stat, stat_halo, o_buf, do_buf, rows,
    acc_kv, acc_q, part_send, part, out,
    s_load, s_in, r_q, r_kv, s_stat, r_stat, s_hstat, r_hstat, s_halo, r_halo,
    s_part, r_part, s_out, r_out,
):
    tokens = q_ref.shape[0]
    groups = 4
    me_c, me_j = lax.axis_index("ctx"), lax.axis_index("head")
    half = ctx_count // 2
    flip = me_c // half
    group = lax.rem(me_j + 2 * flip, groups)
    sides = []
    for step in (ctx_count - 1, 1):
        c = lax.rem(me_c + step, ctx_count)
        sides.append((c, lax.rem(me_j + 2 * flip + 2 * (c // half), groups)))
    peers = [(r, lax.rem(me_j + r, groups), lax.rem(group + r, groups)) for r in (2, 1, 3)]
    my_rows = pl.ds(pl.multiple_of(me_j * tokens, tokens), tokens)

    def columns(which_group, head):
        return pl.ds(pl.multiple_of((which_group * heads + head) * HD, HD), HD)

    def remote(src, dst, send, recv, device):
        pltpu.make_async_remote_copy(
            src_ref=src, dst_ref=dst, send_sem=send, recv_sem=recv,
            device_id=device, device_id_type=MESH,
        ).start()

    def wait_bytes(ref, sem):
        pltpu.make_async_copy(ref, ref, sem).wait()

    load_o = pltpu.make_async_copy(o_ref, o_buf, s_load.at[0])
    load_do = pltpu.make_async_copy(do_ref, do_buf, s_load.at[1])
    load_o.start()
    load_do.start()

    barrier = pltpu.get_barrier_semaphore()
    for _, peer, _ in peers:
        pl.semaphore_signal(barrier, inc=1, device_id=(me_c, peer), device_id_type=MESH)
    for side in sides:
        pl.semaphore_signal(barrier, inc=1, device_id=side, device_id_type=MESH)
    pl.semaphore_wait(barrier, len(peers) + len(sides))

    def send_in(head):
        for first, refs, sem in ((0, (q_ref, do_ref), r_q), (2, (k_ref, v_ref), r_kv)):
            for index, ref in enumerate(refs):
                for _, peer, peer_group in peers:
                    remote(
                        ref.at[:, columns(peer_group, head)],
                        own.at[head, first + index, my_rows],
                        s_in.at[head], sem.at[head], (me_c, peer),
                    )
                pltpu.make_async_copy(
                    ref.at[:, columns(group, head)],
                    own.at[head, first + index, my_rows],
                    sem.at[head],
                ).start()

    for head in range(AHEAD):
        send_in(head)

    load_o.wait()
    load_do.wait()
    all_heads = groups * heads
    lane = lax.broadcasted_iota(jnp.int32, (tokens, HD), 1)
    columns_f = jnp.zeros((tokens, HD), jnp.float32)
    for n in range(all_heads):
        span = slice(n * HD, (n + 1) * HD)
        product = do_buf[:, span].astype(jnp.float32) * o_buf[:, span].astype(jnp.float32)
        columns_f = jnp.where(lane == 32 + n, jnp.sum(product, axis=1, keepdims=True), columns_f)
    rows[...] = columns_f
    rows[:, 0:all_heads] = lse_ref[...] * LOG2E
    turned = rows[...].T
    for g in range(groups):
        stat_send[g] = jnp.zeros((16, tokens), jnp.float32)
        stat_send[g, 0:heads] = turned[g * heads:(g + 1) * heads]
        stat_send[g, 8:8 + heads] = turned[32 + g * heads:32 + (g + 1) * heads]
    stat[me_j] = stat_send[group]
    for _, peer, peer_group in peers:
        remote(stat_send.at[peer_group], stat.at[me_j], s_stat, r_stat, (me_c, peer))

    tiles = 2 * ctx_count

    def tile_at(shift):
        return lax.rem(2 * me_c + shift + tiles, tiles)

    def off_amount(shift_q, shift_k):
        e = shift_k - shift_q + WIN
        s, u = tile_at(shift_q), tile_at(shift_k)
        open_ctx = (cf_ref[s] == 0) | (cf_ref[u] == 1)
        ok = open_ctx if e == WIN else open_ctx & (wm_ref[s, e] == 1)
        return jnp.where(ok, jnp.float32(0.0), jnp.float32(OFF))

    off = {
        (s, u): off_amount(s, u) for s in range(-2, 4) for u in (0, 1) if abs(s - u) <= WIN
    }

    scale = HD ** -0.5

    def stat_row(ref_at, tile, row):
        return jnp.concatenate(
            [ref_at(2 * tile, row), ref_at(2 * tile + 1, row)], axis=1
        )

    def pair(k, v, kt, q, do, lse, delta):
        probs = jnp.exp2(
            lax.dot_general(k, q, NT, preferred_element_type=jnp.float32) * (scale * LOG2E) - lse
        )
        dprobs = lax.dot_general(v, do, NT, preferred_element_type=jnp.float32)
        dscores = (probs * (dprobs - delta)).astype(jnp.bfloat16)
        return (
            matmul(dscores, q),
            matmul(probs.astype(jnp.bfloat16), do),
            matmul(kt, dscores),
        )

    def load_keys(head):
        made = []
        for t in range(2):
            span = pl.ds(t * TILE, TILE)
            k = own[head, 2, span]
            made.append((k, own[head, 3, span], k.T))
        return made

    def own_pairs(head):
        keys = load_keys(head)
        for s in range(2):
            span = pl.ds(s * TILE, TILE)
            q, do = own[head, 0, span], own[head, 1, span]
            row = lambda b, r: stat[b, pl.ds(r, 1)]
            lse, delta = stat_row(row, s, head), stat_row(row, s, head + 8)
            dq = None
            for t in range(2):
                dk, dv, term = pair(*keys[t], q, do, lse + off[s, t], delta)
                if s == 0:
                    acc_kv[0, t], acc_kv[1, t] = dk, dv
                else:
                    acc_kv[0, t] += dk
                    acc_kv[1, t] += dv
                dq = term if dq is None else dq + term
            acc_q[head, s] = dq

    def halo_pairs(head):
        keys = load_keys(head)
        for side in range(2):
            for s in range(2):
                shift = s - 2 if side == 0 else s + 2
                span = pl.ds(s * TILE, TILE)
                q, do = halo[head, side, 0, span], halo[head, side, 1, span]
                row = lambda b, r: stat_halo[side, b, pl.ds(r, 1)]
                lse, delta = stat_row(row, s, head), stat_row(row, s, head + 8)
                dq = None
                for t in range(2):
                    if (shift, t) not in off:
                        continue
                    dk, dv, term = pair(*keys[t], q, do, lse + off[shift, t], delta)
                    acc_kv[0, t] += dk
                    acc_kv[1, t] += dv
                    dq = term if dq is None else dq + term
                part_send[head, side, s] = (dq * scale).astype(jnp.bfloat16)
            remote(
                part_send.at[head, side], part.at[head, 1 - side],
                s_part.at[head], r_part.at[head], sides[side],
            )
        for t in range(2):
            span = pl.ds(t * TILE, TILE)
            out[head, 1, span] = (acc_kv[0, t] * scale).astype(jnp.bfloat16)
            out[head, 2, span] = acc_kv[1, t].astype(jnp.bfloat16)

    outputs = (dq_ref, dk_ref, dv_ref)

    def send_out(head, which):
        for index in which:
            target = outputs[index].at[:, columns(group, head)]
            for _, peer, _ in peers:
                rows_there = pl.ds(pl.multiple_of(peer * tokens, tokens), tokens)
                remote(
                    out.at[head, index, rows_there], target,
                    s_out.at[head], r_out.at[index], (me_c, peer),
                )
            pltpu.make_async_copy(out.at[head, index, my_rows], target, r_out.at[index]).start()

    def finish_q(head):
        for s in range(2):
            total = acc_q[head, s] * scale
            total = total + part[head, 0, s].astype(jnp.float32)
            total = total + part[head, 1, s].astype(jnp.float32)
            out[head, 0, pl.ds(s * TILE, TILE)] = total.T.astype(jnp.bfloat16)

    wait_bytes(stat.at[0:3], r_stat)
    for side in range(2):
        remote(stat, stat_halo.at[1 - side], s_hstat, r_hstat.at[1 - side], sides[side])

    def step(i, carry):
        @pl.when(i + AHEAD < heads)
        def _():
            send_in(i + AHEAD)

        @pl.when(i < heads)
        def _():
            wait_bytes(own.at[i, 0:2], r_q.at[i])
            for side in range(2):
                remote(
                    own.at[i, 0:2], halo.at[i, 1 - side],
                    s_halo.at[i], r_halo.at[i, 1 - side], sides[side],
                )

        @pl.when((i >= 1) & (i <= heads))
        def _():
            head = i - 1
            wait_bytes(own.at[head, 2:4], r_kv.at[head])
            own_pairs(head)
            for side in range(2):
                wait_bytes(halo.at[head, side], r_halo.at[head, side])
            halo_pairs(head)
            send_out(head, (1, 2))

        @pl.when(i >= 2)
        def _():
            head = i - 2
            wait_bytes(part.at[head], r_part.at[head])
            finish_q(head)
            send_out(head, (0,))

        return carry

    for side in range(2):
        wait_bytes(stat_halo.at[side], r_hstat.at[side])
    lax.fori_loop(0, heads + 2, step, 0)

    wait_bytes(stat.at[0:3], s_stat)
    wait_bytes(stat_halo, s_hstat)

    def drain(head, carry):
        wait_bytes(own.at[head, :, pl.ds(0, 3 * tokens)], s_in.at[head])
        wait_bytes(own.at[head], s_halo.at[head])
        wait_bytes(part_send.at[head], s_part.at[head])
        wait_bytes(out.at[head, :, pl.ds(0, 3 * tokens)], s_out.at[head])
        return carry

    lax.fori_loop(0, heads, drain, 0)
    for index in range(3):
        wait_bytes(outputs[index], r_out.at[index])


def per_device(queries, keys, values, outputs, out_grads, log_sums, window_mask, context_flag):
    tokens, width = queries.shape
    ctx_count, groups = lax.axis_size("ctx"), lax.axis_size("head")
    heads = log_sums.shape[1] // groups
    block = groups * tokens
    bf16, f32 = jnp.bfloat16, jnp.float32
    dma, vmem = pltpu.SemaphoreType.DMA, pltpu.VMEM
    anywhere = pl.BlockSpec(memory_space=pl.ANY)
    scalars = pl.BlockSpec(memory_space=pltpu.SMEM)
    return pl.pallas_call(
        functools.partial(kernel, ctx_count, heads),
        out_shape=[jax.ShapeDtypeStruct((tokens, width), bf16)] * 3,
        in_specs=[anywhere] * 5 + [pl.BlockSpec(memory_space=pltpu.VMEM), scalars, scalars],
        out_specs=[anywhere] * 3,
        scratch_shapes=[
            vmem((heads, 4, block, HD), bf16),
            vmem((heads, 2, 2, block, HD), bf16),
            vmem((groups, 16, tokens), f32),
            vmem((groups, 16, tokens), f32),
            vmem((2, groups, 16, tokens), f32),
            vmem((tokens, width), bf16),
            vmem((tokens, width), bf16),
            vmem((tokens, HD), f32),
            vmem((2, 2, TILE, HD), f32),
            vmem((heads, 2, HD, TILE), f32),
            vmem((heads, 2, 2, HD, TILE), bf16),
            vmem((heads, 2, 2, HD, TILE), bf16),
            vmem((heads, 3, block, HD), bf16),
            dma((2,)),
            dma((heads,)),
            dma((heads,)),
            dma((heads,)),
            dma,
            dma,
            dma,
            dma((2,)),
            dma((heads,)),
            dma((heads, 2)),
            dma((heads,)),
            dma((heads,)),
            dma((heads,)),
            dma((3,)),
        ],
        compiler_params=pltpu.CompilerParams(
            collective_id=0, has_side_effects=True, vmem_limit_bytes=40 * 1024 * 1024
        ),
        name="attention_grads",
    )(queries, keys, values, outputs, out_grads, log_sums, window_mask, context_flag)


def solution(mesh):
    placed = (P(("ctx", "head"), None),) * 6 + (P(), P())
    return jax.shard_map(
        per_device,
        mesh=mesh,
        in_specs=placed,
        out_specs=(P(("ctx", "head"), None),) * 3,
        check_vma=False,
    )
```

time: 302 us -> 102 us (0.34)
  the two profiles are of different devices: /device:TPU:36 before, /device:TPU:1 now
where the time goes in v1:
time: 102 us; the launch traced here: 101 us
  Pallas kernels  90.4 us (89%)
  local copies, waits for them, and re-layouts  9.77 us (10%)
    pallas_call x1, Pallas kernels, per_device(): pl.pallas_call(functools.partial(kernel, ctx_count, heads), out_shape=[ja...  90.4 us
    unnamed x19, local copies, waits for them, and re-layouts  9.77 us

profile of v1, /device:TPU:1, one launch (start us, length us, event | category | flops | bytes accessed | tf_op | source)
XLA Modules:
  0.0 100.8 jit_solution(5130546116244725956)
XLA Ops:
  0.6 0.0 copy-start.6
  0.6 0.8 copy.11.lse_ref
  1.5 0.0 copy-done.6
  1.5 0.0 copy-start.5
  1.5 0.1 copy.12.wm_ref
  1.6 0.5 copy-done.5
  2.1 0.0 copy-start
  2.1 1.1 %copy-done = bf16[128,3072]{1,0:T(8,128)(2,1)S(1)} copy-done((bf16[128,3072]{1,0:T(8,128)(2,1)S(1)}, bf16[128,3072]{1,0:T(8,128)(2,1)}, u32[]{:S(2)}) %copy-start) | copy-done | bytes 786456
  3.3 0.0 copy-start.1
  3.3 1.1 %copy-done.1 = bf16[128,3072]{1,0:T(8,128)(2,1)S(1)} copy-done((bf16[128,3072]{1,0:T(8,128)(2,1)S(1)}, bf16[128,3072]{1,0:T(8,128)(2,1)}, u32[]{:S(2)}) %copy-start.1) | copy-done | bytes 786456
  4.4 0.0 copy-start.2
  4.4 1.1 %copy-done.2 = bf16[128,3072]{1,0:T(8,128)(2,1)S(1)} copy-done((bf16[128,3072]{1,0:T(8,128)(2,1)S(1)}, bf16[128,3072]{1,0:T(8,128)(2,1)}, u32[]{:S(2)}) %copy-start.2) | copy-done | bytes 786456
  5.5 0.0 copy-start.3
  5.5 1.1 %copy-done.3 = bf16[128,3072]{1,0:T(8,128)(2,1)S(1)} copy-done((bf16[128,3072]{1,0:T(8,128)(2,1)S(1)}, bf16[128,3072]{1,0:T(8,128)(2,1)}, u32[]{:S(2)}) %copy-start.3) | copy-done | bytes 786456
  6.7 0.0 copy-start.4
  6.7 1.1 %copy-done.4 = bf16[128,3072]{1,0:T(8,128)(2,1)S(1)} copy-done((bf16[128,3072]{1,0:T(8,128)(2,1)S(1)}, bf16[128,3072]{1,0:T(8,128)(2,1)}, u32[]{:S(2)}) %copy-start.4) | copy-done | bytes 786456
  7.8 90.4 %attention_grads.1 = (bf16[128,3072]{1,0:T(8,128)(2,1)S(1)}, bf16[128,3072]{1,0:T(8,128)(2,1)S(1)}, bf16[128,3072]{1,0:T(8,128)(2,1)S(1)}) custom-call(bf16[128,3072]{1,0:T(8,128)(2,1)S(1)} %copy-done, bf16[128,3072]{1,0:T(8,128)(2,1)S(1)} %copy-done.1, bf16[128,3072]{1,0:T(8,128)(2,1)S(1)} %copy-done.2, bf16[128,3072]{1,0:T(8,128)(2,1)S(1)} %copy-done.3, ...), custom_call_target="tpu_custom_call" | custom-call | tf_op jit(solution)/shard_map/attention_grads/pallas_call | solution.py:282
  98.2 0.9 copy.16
  99.0 0.9 copy.17
  99.9 0.9 copy.18
Async XLA Ops:
  0.6 0.8 copy-start.6
  1.5 0.7 copy-start.5
  2.1 1.1 %copy-start = (bf16[128,3072]{1,0:T(8,128)(2,1)S(1)}, bf16[128,3072]{1,0:T(8,128)(2,1)}, u32[]{:S(2)}) copy-start(bf16[128,3072]{1,0:T(8,128)(2,1)} %q_ref.1) | copy-start | bytes 2359300
  3.3 1.1 %copy-start.1 = (bf16[128,3072]{1,0:T(8,128)(2,1)S(1)}, bf16[128,3072]{1,0:T(8,128)(2,1)}, u32[]{:S(2)}) copy-start(bf16[128,3072]{1,0:T(8,128)(2,1)} %k_ref.1) | copy-start | bytes 2359300
  4.4 1.1 %copy-start.2 = (bf16[128,3072]{1,0:T(8,128)(2,1)S(1)}, bf16[128,3072]{1,0:T(8,128)(2,1)}, u32[]{:S(2)}) copy-start(bf16[128,3072]{1,0:T(8,128)(2,1)} %v_ref.1) | copy-start | bytes 2359300
  5.5 1.1 %copy-start.3 = (bf16[128,3072]{1,0:T(8,128)(2,1)S(1)}, bf16[128,3072]{1,0:T(8,128)(2,1)}, u32[]{:S(2)}) copy-start(bf16[128,3072]{1,0:T(8,128)(2,1)} %o_ref.1) | copy-start | bytes 2359300
  6.7 1.1 %copy-start.4 = (bf16[128,3072]{1,0:T(8,128)(2,1)S(1)}, bf16[128,3072]{1,0:T(8,128)(2,1)}, u32[]{:S(2)}) copy-start(bf16[128,3072]{1,0:T(8,128)(2,1)} %do_ref.1) | copy-start | bytes 2359300

commit v2 on v1

--- a/solution.py
+++ b/solution.py
@@ -10,7 +10,6 @@
 TILE = 256
 HD = 128
 WIN = 2
-AHEAD = 2
 LOG2E = 1.4426950408889634
 OFF = 1e30
 MESH = pl.DeviceIdType.MESH
@@ -24,9 +23,9 @@
 def kernel(
     ctx_count,
     heads,
-    q_ref, k_ref, v_ref, o_ref, do_ref, lse_ref, wm_ref, cf_ref,
+    q_ref, k_ref, v_ref, o_ref, do_ref, lse_hbm, wm_hbm, cf_hbm,
     dq_ref, dk_ref, dv_ref,
-    own, halo, stat_send, stat, stat_halo, o_buf, do_buf, rows,
+    own, halo, stat_send, stat, stat_halo, o_buf, do_buf, lse_ref, wm_ref, cf_ref, rows,
     acc_kv, acc_q, part_send, part, out,
     s_load, s_in, r_q, r_kv, s_stat, r_stat, s_hstat, r_hstat, s_halo, r_halo,
     s_part, r_part, s_out, r_out,
@@ -56,10 +55,14 @@
     def wait_bytes(ref, sem):
         pltpu.make_async_copy(ref, ref, sem).wait()
 
-    load_o = pltpu.make_async_copy(o_ref, o_buf, s_load.at[0])
-    load_do = pltpu.make_async_copy(do_ref, do_buf, s_load.at[1])
-    load_o.start()
-    load_do.start()
+    loads = [
+        pltpu.make_async_copy(src, dst, s_load.at[n])
+        for n, (src, dst) in enumerate((
+            (o_ref, o_buf), (do_ref, do_buf), (lse_hbm, lse_ref), (wm_hbm, wm_ref), (cf_hbm, cf_ref),
+        ))
+    ]
+    for load in loads:
+        load.start()
 
     barrier = pltpu.get_barrier_semaphore()
     for _, peer, _ in peers:
@@ -68,40 +71,45 @@
         pl.semaphore_signal(barrier, inc=1, device_id=side, device_id_type=MESH)
     pl.semaphore_wait(barrier, len(peers) + len(sides))
 
-    def send_in(head):
-        for first, refs, sem in ((0, (q_ref, do_ref), r_q), (2, (k_ref, v_ref), r_kv)):
-            for index, ref in enumerate(refs):
-                for _, peer, peer_group in peers:
-                    remote(
-                        ref.at[:, columns(peer_group, head)],
-                        own.at[head, first + index, my_rows],
-                        s_in.at[head], sem.at[head], (me_c, peer),
-                    )
-                pltpu.make_async_copy(
-                    ref.at[:, columns(group, head)],
+    def send_in(head, first, refs, sem):
+        for index, ref in enumerate(refs):
+            for _, peer, peer_group in peers:
+                remote(
+                    ref.at[:, columns(peer_group, head)],
                     own.at[head, first + index, my_rows],
-                    sem.at[head],
-                ).start()
-
-    for head in range(AHEAD):
-        send_in(head)
-
-    load_o.wait()
-    load_do.wait()
+                    s_in.at[head], sem.at[head], (me_c, peer),
+                )
+            pltpu.make_async_copy(
+                ref.at[:, columns(group, head)],
+                own.at[head, first + index, my_rows],
+                sem.at[head],
+            ).start()
+
+    def send_queries(head):
+        send_in(head, 0, (q_ref, do_ref), r_q)
+
+    def send_keys(head):
+        send_in(head, 2, (k_ref, v_ref), r_kv)
+
+    send_queries(0)
+
+    for load in loads:
+        load.wait()
     all_heads = groups * heads
     lane = lax.broadcasted_iota(jnp.int32, (tokens, HD), 1)
     columns_f = jnp.zeros((tokens, HD), jnp.float32)
     for n in range(all_heads):
         span = slice(n * HD, (n + 1) * HD)
         product = do_buf[:, span].astype(jnp.float32) * o_buf[:, span].astype(jnp.float32)
-        columns_f = jnp.where(lane == 32 + n, jnp.sum(product, axis=1, keepdims=True), columns_f)
+        columns_f = jnp.where(lane == n, jnp.sum(product, axis=1, keepdims=True), columns_f)
     rows[...] = columns_f
-    rows[:, 0:all_heads] = lse_ref[...] * LOG2E
     turned = rows[...].T
+    send_keys(0)
+    send_queries(1)
     for g in range(groups):
         stat_send[g] = jnp.zeros((16, tokens), jnp.float32)
-        stat_send[g, 0:heads] = turned[g * heads:(g + 1) * heads]
-        stat_send[g, 8:8 + heads] = turned[32 + g * heads:32 + (g + 1) * heads]
+        stat_send[g, 0:heads] = lse_ref[g * heads:(g + 1) * heads] * LOG2E
+        stat_send[g, 8:8 + heads] = turned[g * heads:(g + 1) * heads]
     stat[me_j] = stat_send[group]
     for _, peer, peer_group in peers:
         remote(stat_send.at[peer_group], stat.at[me_j], s_stat, r_stat, (me_c, peer))
@@ -115,7 +123,7 @@
         e = shift_k - shift_q + WIN
         s, u = tile_at(shift_q), tile_at(shift_k)
         open_ctx = (cf_ref[s] == 0) | (cf_ref[u] == 1)
-        ok = open_ctx if e == WIN else open_ctx & (wm_ref[s, e] == 1)
+        ok = open_ctx if e == WIN else open_ctx & (wm_ref[e, s] == 1)
         return jnp.where(ok, jnp.float32(0.0), jnp.float32(OFF))
 
     off = {
@@ -214,15 +222,7 @@
             total = total + part[head, 1, s].astype(jnp.float32)
             out[head, 0, pl.ds(s * TILE, TILE)] = total.T.astype(jnp.bfloat16)
 
-    wait_bytes(stat.at[0:3], r_stat)
-    for side in range(2):
-        remote(stat, stat_halo.at[1 - side], s_hstat, r_hstat.at[1 - side], sides[side])
-
     def step(i, carry):
-        @pl.when(i + AHEAD < heads)
-        def _():
-            send_in(i + AHEAD)
-
         @pl.when(i < heads)
         def _():
             wait_bytes(own.at[i, 0:2], r_q.at[i])
@@ -231,6 +231,25 @@
                     own.at[i, 0:2], halo.at[i, 1 - side],
                     s_halo.at[i], r_halo.at[i, 1 - side], sides[side],
                 )
+
+        @pl.when(i + 1 < heads)
+        def _():
+            send_keys(i + 1)
+
+        @pl.when(i + 2 < heads)
+        def _():
+            send_queries(i + 2)
+
+        @pl.when(i == 0)
+        def _():
+            wait_bytes(stat.at[0:3], r_stat)
+            for side in range(2):
+                remote(stat, stat_halo.at[1 - side], s_hstat, r_hstat.at[1 - side], sides[side])
+
+        @pl.when(i == 1)
+        def _():
+            for side in range(2):
+                wait_bytes(stat_halo.at[side], r_hstat.at[side])
 
         @pl.when((i >= 1) & (i <= heads))
         def _():
@@ -251,8 +270,6 @@
 
         return carry
 
-    for side in range(2):
-        wait_bytes(stat_halo.at[side], r_hstat.at[side])
     lax.fori_loop(0, heads + 2, step, 0)
 
     wait_bytes(stat.at[0:3], s_stat)
@@ -268,6 +285,22 @@
     lax.fori_loop(0, heads, drain, 0)
     for index in range(3):
         wait_bytes(outputs[index], r_out.at[index])
+
+
+def copy_out(*refs):
+    buf, sems = refs[6], refs[7]
+    parts = 4
+    size = refs[0].shape[0] // parts
+    steps = [(n, p, pl.ds(p * size, size)) for p in range(parts) for n in range(3)]
+    ins = [pltpu.make_async_copy(refs[n].at[r], buf.at[n, r], sems.at[0, n, p]) for n, p, r in steps]
+    outs = [pltpu.make_async_copy(buf.at[n, r], refs[3 + n].at[r], sems.at[1, n, p]) for n, p, r in steps]
+    for copy in ins:
+        copy.start()
+    for first, second in zip(ins, outs):
+        first.wait()
+        second.start()
+    for copy in outs:
+        copy.wait()
 
 
 def per_device(queries, keys, values, outputs, out_grads, log_sums, window_mask, context_flag):
@@ -278,11 +311,10 @@
     bf16, f32 = jnp.bfloat16, jnp.float32
     dma, vmem = pltpu.SemaphoreType.DMA, pltpu.VMEM
     anywhere = pl.BlockSpec(memory_space=pl.ANY)
-    scalars = pl.BlockSpec(memory_space=pltpu.SMEM)
-    return pl.pallas_call(
+    grads = pl.pallas_call(
         functools.partial(kernel, ctx_count, heads),
         out_shape=[jax.ShapeDtypeStruct((tokens, width), bf16)] * 3,
-        in_specs=[anywhere] * 5 + [pl.BlockSpec(memory_space=pltpu.VMEM), scalars, scalars],
+        in_specs=[anywhere] * 8,
         out_specs=[anywhere] * 3,
         scratch_shapes=[
             vmem((heads, 4, block, HD), bf16),
@@ -292,13 +324,16 @@
             vmem((2, groups, 16, tokens), f32),
             vmem((tokens, width), bf16),
             vmem((tokens, width), bf16),
+            vmem(log_sums.shape[::-1], f32),
+            pltpu.SMEM(window_mask.shape[::-1], jnp.int32),
+            pltpu.SMEM(context_flag.shape, jnp.int32),
             vmem((tokens, HD), f32),
             vmem((2, 2, TILE, HD), f32),
             vmem((heads, 2, HD, TILE), f32),
             vmem((heads, 2, 2, HD, TILE), bf16),
             vmem((heads, 2, 2, HD, TILE), bf16),
             vmem((heads, 3, block, HD), bf16),
-            dma((2,)),
+            dma((5,)),
             dma((heads,)),
             dma((heads,)),
             dma((heads,)),
@@ -314,10 +349,18 @@
             dma((3,)),
         ],
         compiler_params=pltpu.CompilerParams(
-            collective_id=0, has_side_effects=True, vmem_limit_bytes=40 * 1024 * 1024
+            collective_id=0, has_side_effects=True, vmem_limit_bytes=60 * 1024 * 1024
         ),
         name="attention_grads",
-    )(queries, keys, values, outputs, out_grads, log_sums, window_mask, context_flag)
+    )(queries, keys, values, outputs, out_grads, log_sums.T, window_mask.T, context_flag)
+    return pl.pallas_call(
+        copy_out,
+        out_shape=[jax.ShapeDtypeStruct((tokens, width), bf16)] * 3,
+        in_specs=[anywhere] * 3,
+        out_specs=[anywhere] * 3,
+        scratch_shapes=[vmem((3, tokens, width), bf16), dma((2, 3, 4))],
+        name="results_out",
+    )(*grads)
 
 
 def solution(mesh):

time: 102 us -> 83 us (0.81); the launches traced: 101 us -> 82.9 us
  local copies, waits for them, and re-layouts: 9.77 us -> 0 us
  Pallas kernels: 90.4 us -> 82.3 us
    pallas_call x1, Pallas kernels: 90.4 us -> 79.6 us  [per_device(): pl.pallas_call(functools.partial(kernel, ctx_count, heads), out_shape=[ja...]
    unnamed x19 -> x0, local copies, waits for them, and re-layouts: 9.77 us -> none
    pallas_call x0 -> x1, Pallas kernels: none -> 2.62 us  [per_device(): pl.pallas_call(copy_out, out_shape=[jax.ShapeDtypeStruct((tokens, width),...]
where the time goes in v2:
time: 83 us; the launch traced here: 82.9 us
  Pallas kernels  82.3 us (99%)
    pallas_call x1, Pallas kernels, per_device(): pl.pallas_call(functools.partial(kernel, ctx_count, heads), out_shape=[ja...  79.6 us
    pallas_call x1, Pallas kernels, per_device(): pl.pallas_call(copy_out, out_shape=[jax.ShapeDtypeStruct((tokens, width),...  2.62 us

profile of v2, /device:TPU:1, one launch (start us, length us, event | category | flops | bytes accessed | tf_op | source)
XLA Modules:
  0.0 82.9 jit_solution(11122576644655419115)
XLA Ops:
  0.6 79.6 %attention_grads.1 = (bf16[128,3072]{1,0:T(8,128)(2,1)}, bf16[128,3072]{1,0:T(8,128)(2,1)}, bf16[128,3072]{1,0:T(8,128)(2,1)}) custom-call(bf16[128,3072]{1,0:T(8,128)(2,1)} %q_ref.1, bf16[128,3072]{1,0:T(8,128)(2,1)} %k_ref.1, bf16[128,3072]{1,0:T(8,128)(2,1)} %v_ref.1, bf16[128,3072]{1,0:T(8,128)(2,1)} %o_ref.1, bf16[128,3072]{1,0:T(8,128)(2,1)} %do_ref.1, ...), custom_call_target="tpu_custom_call" | custom-call | tf_op jit(solution)/shard_map/attention_grads/pallas_call | solution.py:314
  80.3 2.6 %results_out.1 = (bf16[128,3072]{1,0:T(8,128)(2,1)}, bf16[128,3072]{1,0:T(8,128)(2,1)}, bf16[128,3072]{1,0:T(8,128)(2,1)}) custom-call(bf16[128,3072]{1,0:T(8,128)(2,1)} %get-tuple-element.6.refs_0_, bf16[128,3072]{1,0:T(8,128)(2,1)} %get-tuple-element.7.refs_1_, bf16[128,3072]{1,0:T(8,128)(2,1)} %get-tuple-element.8.refs_2_), custom_call_target="tpu_custom_call" | custom-call | tf_op jit(solution)/shard_map/results_out/pallas_call | solution.py:356

commit v3 on v2

--- a/solution.py
+++ b/solution.py
@@ -12,6 +12,7 @@
 WIN = 2
 LOG2E = 1.4426950408889634
 OFF = 1e30
+FIRST_DELTAS = 10
 MESH = pl.DeviceIdType.MESH
 NT = (((1,), (1,)), ((), ()))
 
@@ -28,7 +29,7 @@
     own, halo, stat_send, stat, stat_halo, o_buf, do_buf, lse_ref, wm_ref, cf_ref, rows,
     acc_kv, acc_q, part_send, part, out,
     s_load, s_in, r_q, r_kv, s_stat, r_stat, s_hstat, r_hstat, s_halo, r_halo,
-    s_part, r_part, s_out, r_out,
+    s_part, r_part, s_out, r_out, gate,
 ):
     tokens = q_ref.shape[0]
     groups = 4
@@ -64,12 +65,40 @@
     for load in loads:
         load.start()
 
+    leader = groups - 1
     barrier = pltpu.get_barrier_semaphore()
-    for _, peer, _ in peers:
-        pl.semaphore_signal(barrier, inc=1, device_id=(me_c, peer), device_id_type=MESH)
-    for side in sides:
-        pl.semaphore_signal(barrier, inc=1, device_id=side, device_id_type=MESH)
-    pl.semaphore_wait(barrier, len(peers) + len(sides))
+    for _, peer, peer_group in peers:
+        @pl.when(peer_group != leader)
+        def _():
+            pl.semaphore_signal(barrier, inc=1, device_id=(me_c, peer), device_id_type=MESH)
+
+    for c, _ in sides:
+        side_leader = lax.rem(leader + 2 * (c // half), groups)
+        pl.semaphore_signal(barrier, inc=1, device_id=(c, side_leader), device_id_type=MESH)
+
+    @pl.when(group != leader)
+    def _():
+        pl.semaphore_wait(barrier, len(peers))
+
+    for _, peer, peer_group in peers:
+        @pl.when(peer_group == leader)
+        def _():
+            pl.semaphore_signal(gate, inc=1, device_id=(me_c, peer), device_id_type=MESH)
+
+    @pl.when(group == leader)
+    def _():
+        pl.semaphore_wait(gate, len(peers))
+
+    def meet_sides():
+        @pl.when(group == leader)
+        def _():
+            pl.semaphore_wait(barrier, len(sides) * groups)
+            for _, peer, _ in peers:
+                pl.semaphore_signal(gate, inc=1, device_id=(me_c, peer), device_id_type=MESH)
+
+        @pl.when(group != leader)
+        def _():
+            pl.semaphore_wait(gate, 1)
 
     def send_in(head, first, refs, sem):
         for index, ref in enumerate(refs):
@@ -93,19 +122,48 @@
 
     send_queries(0)
 
+    partner_rows = pl.ds(pl.multiple_of((1 - me_j // 2) * TILE, TILE), TILE)
+
+    def send_halo_direct(head):
+        for index, ref in enumerate((q_ref, do_ref)):
+            for core in range(2):
+                their_group = group + core * (1 - 2 * lax.rem(group, 2))
+                for side, (c, j) in enumerate(sides):
+                    remote(
+                        ref.at[:, columns(their_group, head)],
+                        halo.at[head, 1 - side, index, my_rows],
+                        s_halo.at[head], r_halo.at[head, 1 - side],
+                        (c, j + core * (1 - 2 * lax.rem(j, 2))),
+                    )
+
+    def send_halo(head):
+        wait_bytes(own.at[head, 0:2], r_q.at[head])
+        for side in range(2):
+            remote(
+                own.at[head, 0:2, partner_rows], halo.at[head, 1 - side, :, partner_rows],
+                s_halo.at[head], r_halo.at[head, 1 - side], sides[side],
+            )
+
+    all_heads = groups * heads
+    lane = lax.broadcasted_iota(jnp.int32, (tokens, HD), 1)
+
+    def add_deltas(columns_f, first, last):
+        for n in range(first, last):
+            span = slice(n * HD, (n + 1) * HD)
+            product = do_buf[:, span].astype(jnp.float32) * o_buf[:, span].astype(jnp.float32)
+            columns_f = jnp.where(lane == n, jnp.sum(product, axis=1, keepdims=True), columns_f)
+        return columns_f
+
     for load in loads:
         load.wait()
-    all_heads = groups * heads
-    lane = lax.broadcasted_iota(jnp.int32, (tokens, HD), 1)
-    columns_f = jnp.zeros((tokens, HD), jnp.float32)
-    for n in range(all_heads):
-        span = slice(n * HD, (n + 1) * HD)
-        product = do_buf[:, span].astype(jnp.float32) * o_buf[:, span].astype(jnp.float32)
-        columns_f = jnp.where(lane == n, jnp.sum(product, axis=1, keepdims=True), columns_f)
-    rows[...] = columns_f
-    turned = rows[...].T
+    rows[...] = add_deltas(jnp.zeros((tokens, HD), jnp.float32), 0, FIRST_DELTAS)
     send_keys(0)
+    meet_sides()
+    send_halo_direct(0)
+    send_halo(0)
+    send_halo_direct(1)
     send_queries(1)
+    turned = add_deltas(rows[...], FIRST_DELTAS, all_heads).T
     for g in range(groups):
         stat_send[g] = jnp.zeros((16, tokens), jnp.float32)
         stat_send[g, 0:heads] = lse_ref[g * heads:(g + 1) * heads] * LOG2E
@@ -113,6 +171,11 @@
     stat[me_j] = stat_send[group]
     for _, peer, peer_group in peers:
         remote(stat_send.at[peer_group], stat.at[me_j], s_stat, r_stat, (me_c, peer))
+    send_keys(1)
+    send_queries(2)
+    wait_bytes(stat.at[0:3], r_stat)
+    for side in range(2):
+        remote(stat, stat_halo.at[1 - side], s_hstat, r_hstat.at[1 - side], sides[side])
 
     tiles = 2 * ctx_count
 
@@ -193,10 +256,10 @@
                     acc_kv[1, t] += dv
                     dq = term if dq is None else dq + term
                 part_send[head, side, s] = (dq * scale).astype(jnp.bfloat16)
-            remote(
-                part_send.at[head, side], part.at[head, 1 - side],
-                s_part.at[head], r_part.at[head], sides[side],
-            )
+                remote(
+                    part_send.at[head, side, s], part.at[head, 1 - side, s],
+                    s_part.at[head], r_part.at[head, s], sides[side],
+                )
         for t in range(2):
             span = pl.ds(t * TILE, TILE)
             out[head, 1, span] = (acc_kv[0, t] * scale).astype(jnp.bfloat16)
@@ -217,41 +280,46 @@
 
     def finish_q(head):
         for s in range(2):
+            wait_bytes(part.at[head, :, s], r_part.at[head, s])
             total = acc_q[head, s] * scale
             total = total + part[head, 0, s].astype(jnp.float32)
             total = total + part[head, 1, s].astype(jnp.float32)
             out[head, 0, pl.ds(s * TILE, TILE)] = total.T.astype(jnp.bfloat16)
+            target = outputs[0].at[:, columns(group, head)]
+            for peer in (2 * s, 2 * s + 1):
+                source = out.at[head, 0, pl.ds(peer * tokens, tokens)]
+
+                @pl.when(peer != me_j)
+                def _():
+                    remote(source, target, s_out.at[head], r_out.at[0], (me_c, peer))
+
+                @pl.when(peer == me_j)
+                def _():
+                    pltpu.make_async_copy(source, target, r_out.at[0]).start()
 
     def step(i, carry):
         @pl.when(i < heads)
         def _():
-            wait_bytes(own.at[i, 0:2], r_q.at[i])
-            for side in range(2):
-                remote(
-                    own.at[i, 0:2], halo.at[i, 1 - side],
-                    s_halo.at[i], r_halo.at[i, 1 - side], sides[side],
-                )
+            send_halo(i)
 
         @pl.when(i + 1 < heads)
         def _():
+            send_halo_direct(i + 1)
+
+        @pl.when(i + 1 < heads)
+        def _():
             send_keys(i + 1)
 
         @pl.when(i + 2 < heads)
         def _():
             send_queries(i + 2)
-
-        @pl.when(i == 0)
-        def _():
-            wait_bytes(stat.at[0:3], r_stat)
-            for side in range(2):
-                remote(stat, stat_halo.at[1 - side], s_hstat, r_hstat.at[1 - side], sides[side])
 
         @pl.when(i == 1)
         def _():
             for side in range(2):
                 wait_bytes(stat_halo.at[side], r_hstat.at[side])
 
-        @pl.when((i >= 1) & (i <= heads))
+        @pl.when(i <= heads)
         def _():
             head = i - 1
             wait_bytes(own.at[head, 2:4], r_kv.at[head])
@@ -264,13 +332,11 @@
         @pl.when(i >= 2)
         def _():
             head = i - 2
-            wait_bytes(part.at[head], r_part.at[head])
             finish_q(head)
-            send_out(head, (0,))
 
         return carry
 
-    lax.fori_loop(0, heads + 2, step, 0)
+    lax.fori_loop(1, heads + 2, step, 0)
 
     wait_bytes(stat.at[0:3], s_stat)
     wait_bytes(stat_halo, s_hstat)
@@ -344,9 +410,10 @@
             dma((heads,)),
             dma((heads, 2)),
             dma((heads,)),
-            dma((heads,)),
+            dma((heads, 2)),
             dma((heads,)),
             dma((3,)),
+            pltpu.SemaphoreType.REGULAR,
         ],
         compiler_params=pltpu.CompilerParams(
             collective_id=0, has_side_effects=True, vmem_limit_bytes=60 * 1024 * 1024

time: 83 us -> 78.7 us (0.948); the launches traced: 82.9 us -> 77.4 us
  Pallas kernels: 82.3 us -> 76.7 us
    pallas_call x1, Pallas kernels: 79.6 us -> 74.1 us  [per_device(): pl.pallas_call(functools.partial(kernel, ctx_count, heads), out_shape=[ja...]
where the time goes in v3:
time: 78.7 us; the launch traced here: 77.4 us
  Pallas kernels  76.7 us (97%)
    pallas_call x1, Pallas kernels, per_device(): pl.pallas_call(functools.partial(kernel, ctx_count, heads), out_shape=[ja...  74.1 us
    pallas_call x1, Pallas kernels, per_device(): pl.pallas_call(copy_out, out_shape=[jax.ShapeDtypeStruct((tokens, width),...  2.62 us

profile of v3, /device:TPU:1, one launch (start us, length us, event | category | flops | bytes accessed | tf_op | source)
XLA Modules:
  0.0 77.4 jit_solution(11713431608225570915)
XLA Ops:
  0.6 74.1 %attention_grads.1 = (bf16[128,3072]{1,0:T(8,128)(2,1)}, bf16[128,3072]{1,0:T(8,128)(2,1)}, bf16[128,3072]{1,0:T(8,128)(2,1)}) custom-call(bf16[128,3072]{1,0:T(8,128)(2,1)} %q_ref.1, bf16[128,3072]{1,0:T(8,128)(2,1)} %k_ref.1, bf16[128,3072]{1,0:T(8,128)(2,1)} %v_ref.1, bf16[128,3072]{1,0:T(8,128)(2,1)} %o_ref.1, bf16[128,3072]{1,0:T(8,128)(2,1)} %do_ref.1, ...), custom_call_target="tpu_custom_call" | custom-call | tf_op jit(solution)/shard_map/attention_grads/pallas_call | solution.py:380
  74.8 2.6 %results_out.1 = (bf16[128,3072]{1,0:T(8,128)(2,1)}, bf16[128,3072]{1,0:T(8,128)(2,1)}, bf16[128,3072]{1,0:T(8,128)(2,1)}) custom-call(bf16[128,3072]{1,0:T(8,128)(2,1)} %get-tuple-element.6.refs_0_, bf16[128,3072]{1,0:T(8,128)(2,1)} %get-tuple-element.7.refs_1_, bf16[128,3072]{1,0:T(8,128)(2,1)} %get-tuple-element.8.refs_2_), custom_call_target="tpu_custom_call" | custom-call | tf_op jit(solution)/shard_map/results_out/pallas_call | solution.py:423

commit v4 on v3

--- a/solution.py
+++ b/solution.py
@@ -161,8 +161,8 @@
     meet_sides()
     send_halo_direct(0)
     send_halo(0)
+    send_queries(1)
     send_halo_direct(1)
-    send_queries(1)
     turned = add_deltas(rows[...], FIRST_DELTAS, all_heads).T
     for g in range(groups):
         stat_send[g] = jnp.zeros((16, tokens), jnp.float32)
@@ -171,8 +171,11 @@
     stat[me_j] = stat_send[group]
     for _, peer, peer_group in peers:
         remote(stat_send.at[peer_group], stat.at[me_j], s_stat, r_stat, (me_c, peer))
+    send_queries(2)
+    send_halo(1)
+    send_halo_direct(2)
     send_keys(1)
-    send_queries(2)
+    send_queries(3)
     wait_bytes(stat.at[0:3], r_stat)
     for side in range(2):
         remote(stat, stat_halo.at[1 - side], s_hstat, r_hstat.at[1 - side], sides[side])
@@ -298,21 +301,18 @@
                     pltpu.make_async_copy(source, target, r_out.at[0]).start()
 
     def step(i, carry):
-        @pl.when(i < heads)
-        def _():
-            send_halo(i)
-
         @pl.when(i + 1 < heads)
         def _():
-            send_halo_direct(i + 1)
-
-        @pl.when(i + 1 < heads)
-        def _():
+            send_halo(i + 1)
             send_keys(i + 1)
 
         @pl.when(i + 2 < heads)
         def _():
-            send_queries(i + 2)
+            send_halo_direct(i + 2)
+
+        @pl.when(i + 3 < heads)
+        def _():
+            send_queries(i + 3)
 
         @pl.when(i == 1)
         def _():
@@ -329,14 +329,14 @@
             halo_pairs(head)
             send_out(head, (1, 2))
 
-        @pl.when(i >= 2)
-        def _():
-            head = i - 2
+        @pl.when(i >= 3)
+        def _():
+            head = i - 3
             finish_q(head)
 
         return carry
 
-    lax.fori_loop(1, heads + 2, step, 0)
+    lax.fori_loop(1, heads + 3, step, 0)
 
     wait_bytes(stat.at[0:3], s_stat)
     wait_bytes(stat_halo, s_hstat)
@@ -354,18 +354,11 @@
 
 
 def copy_out(*refs):
-    buf, sems = refs[6], refs[7]
-    parts = 4
-    size = refs[0].shape[0] // parts
-    steps = [(n, p, pl.ds(p * size, size)) for p in range(parts) for n in range(3)]
-    ins = [pltpu.make_async_copy(refs[n].at[r], buf.at[n, r], sems.at[0, n, p]) for n, p, r in steps]
-    outs = [pltpu.make_async_copy(buf.at[n, r], refs[3 + n].at[r], sems.at[1, n, p]) for n, p, r in steps]
-    for copy in ins:
+    sems = refs[6]
+    copies = [pltpu.make_async_copy(refs[n], refs[3 + n], sems.at[n]) for n in range(3)]
+    for copy in copies:
         copy.start()
-    for first, second in zip(ins, outs):
-        first.wait()
-        second.start()
-    for copy in outs:
+    for copy in copies:
         copy.wait()
 
 
@@ -379,7 +372,7 @@
     anywhere = pl.BlockSpec(memory_space=pl.ANY)
     grads = pl.pallas_call(
         functools.partial(kernel, ctx_count, heads),
-        out_shape=[jax.ShapeDtypeStruct((tokens, width), bf16)] * 3,
+        out_shape=[vmem((tokens, width), bf16)] * 3,
         in_specs=[anywhere] * 8,
         out_specs=[anywhere] * 3,
         scratch_shapes=[
@@ -423,9 +416,10 @@
     return pl.pallas_call(
         copy_out,
         out_shape=[jax.ShapeDtypeStruct((tokens, width), bf16)] * 3,
-        in_specs=[anywhere] * 3,
+        in_specs=[pl.BlockSpec(memory_space=pltpu.VMEM)] * 3,
         out_specs=[anywhere] * 3,
-        scratch_shapes=[vmem((3, tokens, width), bf16), dma((2, 3, 4))],
+        scratch_shapes=[dma((3,))],
+        compiler_params=pltpu.CompilerParams(vmem_limit_bytes=8 * 1024 * 1024),
         name="results_out",
     )(*grads)
 

time: 78.7 us -> 75.2 us (0.956); the launches traced: 77.4 us -> 75.1 us
  Pallas kernels: 76.7 us -> 74.5 us
    pallas_call x1, Pallas kernels: 2.62 us -> 1.43 us  [per_device(): pl.pallas_call(copy_out, out_shape=[jax.ShapeDtypeStruct((tokens, width),...]
    pallas_call x1, Pallas kernels: 74.1 us -> 73 us  [per_device(): pl.pallas_call(functools.partial(kernel, ctx_count, heads), out_shape=[vm...]
where the time goes in v4:
time: 75.2 us; the launch traced here: 75.1 us
  Pallas kernels  74.5 us (99%)
    pallas_call x1, Pallas kernels, per_device(): pl.pallas_call(functools.partial(kernel, ctx_count, heads), out_shape=[vm...  73 us

profile of v4, /device:TPU:1, one launch (start us, length us, event | category | flops | bytes accessed | tf_op | source)
XLA Modules:
  0.0 75.1 jit_solution(13854880670380583817)
XLA Ops:
  0.6 73.0 %attention_grads.1 = (bf16[128,3072]{1,0:T(8,128)(2,1)S(1)}, bf16[128,3072]{1,0:T(8,128)(2,1)S(1)}, bf16[128,3072]{1,0:T(8,128)(2,1)S(1)}) custom-call(bf16[128,3072]{1,0:T(8,128)(2,1)} %q_ref.1, bf16[128,3072]{1,0:T(8,128)(2,1)} %k_ref.1, bf16[128,3072]{1,0:T(8,128)(2,1)} %v_ref.1, bf16[128,3072]{1,0:T(8,128)(2,1)} %o_ref.1, bf16[128,3072]{1,0:T(8,128)(2,1)} %do_ref.1, ...), custom_call_target="tpu_custom_call" | custom-call | tf_op jit(solution)/shard_map/attention_grads/pallas_call | solution.py:373
  73.7 1.4 %results_out.1 = (bf16[128,3072]{1,0:T(8,128)(2,1)}, bf16[128,3072]{1,0:T(8,128)(2,1)}, bf16[128,3072]{1,0:T(8,128)(2,1)}) custom-call(bf16[128,3072]{1,0:T(8,128)(2,1)S(1)} %get-tuple-element.6.refs_0_, bf16[128,3072]{1,0:T(8,128)(2,1)S(1)} %get-tuple-element.7.refs_1_, bf16[128,3072]{1,0:T(8,128)(2,1)S(1)} %get-tuple-element.8.refs_2_), custom_call_target="tpu_custom_call" | custom-call | tf_op jit(solution)/shard_map/results_out/pallas_call | solution.py:416

commit v5 on v4

--- a/solution.py
+++ b/solution.py
@@ -163,6 +163,7 @@
     send_halo(0)
     send_queries(1)
     send_halo_direct(1)
+    send_halo_direct(2)
     turned = add_deltas(rows[...], FIRST_DELTAS, all_heads).T
     for g in range(groups):
         stat_send[g] = jnp.zeros((16, tokens), jnp.float32)
@@ -173,7 +174,6 @@
         remote(stat_send.at[peer_group], stat.at[me_j], s_stat, r_stat, (me_c, peer))
     send_queries(2)
     send_halo(1)
-    send_halo_direct(2)
     send_keys(1)
     send_queries(3)
     wait_bytes(stat.at[0:3], r_stat)
@@ -233,17 +233,18 @@
             dq = None
             for t in range(2):
                 dk, dv, term = pair(*keys[t], q, do, lse + off[s, t], delta)
-                if s == 0:
-                    acc_kv[0, t], acc_kv[1, t] = dk, dv
-                else:
-                    acc_kv[0, t] += dk
-                    acc_kv[1, t] += dv
+                acc_kv[0, t] += dk
+                acc_kv[1, t] += dv
                 dq = term if dq is None else dq + term
             acc_q[head, s] = dq
+        for t in range(2):
+            span = pl.ds(t * TILE, TILE)
+            out[head, 1, span] = (acc_kv[0, t] * scale).astype(jnp.bfloat16)
+            out[head, 2, span] = acc_kv[1, t].astype(jnp.bfloat16)
 
     def halo_pairs(head):
         keys = load_keys(head)
-        for side in range(2):
+        for side in (1, 0):
             for s in range(2):
                 shift = s - 2 if side == 0 else s + 2
                 span = pl.ds(s * TILE, TILE)
@@ -255,18 +256,17 @@
                     if (shift, t) not in off:
                         continue
                     dk, dv, term = pair(*keys[t], q, do, lse + off[shift, t], delta)
-                    acc_kv[0, t] += dk
-                    acc_kv[1, t] += dv
+                    if (side, s) == (1, 0):
+                        acc_kv[0, t], acc_kv[1, t] = dk, dv
+                    else:
+                        acc_kv[0, t] += dk
+                        acc_kv[1, t] += dv
                     dq = term if dq is None else dq + term
                 part_send[head, side, s] = (dq * scale).astype(jnp.bfloat16)
                 remote(
                     part_send.at[head, side, s], part.at[head, 1 - side, s],
                     s_part.at[head], r_part.at[head, s], sides[side],
                 )
-        for t in range(2):
-            span = pl.ds(t * TILE, TILE)
-            out[head, 1, span] = (acc_kv[0, t] * scale).astype(jnp.bfloat16)
-            out[head, 2, span] = acc_kv[1, t].astype(jnp.bfloat16)
 
     outputs = (dq_ref, dk_ref, dv_ref)
 
@@ -323,10 +323,10 @@
         def _():
             head = i - 1
             wait_bytes(own.at[head, 2:4], r_kv.at[head])
-            own_pairs(head)
             for side in range(2):
                 wait_bytes(halo.at[head, side], r_halo.at[head, side])
             halo_pairs(head)
+            own_pairs(head)
             send_out(head, (1, 2))
 
         @pl.when(i >= 3)

time: 75.2 us -> 74.8 us (level)
  no operation moved by 1% of the time
where the time goes in v5:
time: 74.8 us; the launch traced here: 74.7 us
  Pallas kernels  74 us (99%)
    pallas_call x1, Pallas kernels, per_device(): pl.pallas_call(functools.partial(kernel, ctx_count, heads), out_shape=[vm...  72.6 us

profile of v5, /device:TPU:1, one launch (start us, length us, event | category | flops | bytes accessed | tf_op | source)
XLA Modules:
  0.0 74.7 jit_solution(13925609877111200636)
XLA Ops:
  0.6 72.6 %attention_grads.1 = (bf16[128,3072]{1,0:T(8,128)(2,1)S(1)}, bf16[128,3072]{1,0:T(8,128)(2,1)S(1)}, bf16[128,3072]{1,0:T(8,128)(2,1)S(1)}) custom-call(bf16[128,3072]{1,0:T(8,128)(2,1)} %q_ref.1, bf16[128,3072]{1,0:T(8,128)(2,1)} %k_ref.1, bf16[128,3072]{1,0:T(8,128)(2,1)} %v_ref.1, bf16[128,3072]{1,0:T(8,128)(2,1)} %o_ref.1, bf16[128,3072]{1,0:T(8,128)(2,1)} %do_ref.1, ...), custom_call_target="tpu_custom_call" | custom-call | tf_op jit(solution)/shard_map/attention_grads/pallas_call | solution.py:373
  73.3 1.4 %results_out.1 = (bf16[128,3072]{1,0:T(8,128)(2,1)}, bf16[128,3072]{1,0:T(8,128)(2,1)}, bf16[128,3072]{1,0:T(8,128)(2,1)}) custom-call(bf16[128,3072]{1,0:T(8,128)(2,1)S(1)} %get-tuple-element.6.refs_0_, bf16[128,3072]{1,0:T(8,128)(2,1)S(1)} %get-tuple-element.7.refs_1_, bf16[128,3072]{1,0:T(8,128)(2,1)S(1)} %get-tuple-element.8.refs_2_), custom_call_target="tpu_custom_call" | custom-call | tf_op jit(solution)/shard_map/results_out/pallas_call | solution.py:416
